TPU v7x, 256 devices: a whole 4x4x8 slice. The times are simulated.
256 devices in a mesh: img: 16 (over y, x_hi, core), ori: 16 (over z, x_lo).
Axes of the slice: x: 4 (x_hi: 2, x_lo: 2; x = x_hi * 2 + x_lo), y: 4, z: 8, core: 2. Of those that a mesh axis runs over, the one named last changes fastest.
Arguments:
- images: bfloat16 [8192, 4096], P('img'), may hold values from -6 to 6
- ctf_class: int32 [8192], P('img'), may hold values from 0 to 15
- class_mask: int32 [8192, 8], P('img'), may hold values from 0 to 1, as said below
- precision: float32 [8192], P('img'), may hold values from 0.02 to 0.5
- class_log_prior: float32 [8192, 8], P('img'), may hold values from -6 to 406
- ctf_filters: float32 [16, 4096], replicated, may hold values from -1 to 1
- volume_coef: bfloat16 [8, 16, 2, 4096], P(None, 'img'), may hold values from -6 to 6
- slice_ops: bfloat16 [8, 4096, 64], replicated, may hold values from -0.09375 to 0.09375
- tilt_index: int32 [256], P('ori'), may hold values from 0 to 7
- azimuth_index: int32 [256], P('ori'), may hold values from 0 to 31
Outputs:
- coef_sum: float32 [8, 16, 2, 4096], P(None, 'img')
- log_evidence: float32 [8192], P('img')
- class_posterior: float32 [8192, 8], P('img')
Inputs may be any that keep to these rules, and one draw needn't show every extreme that they name: `class_mask`: every image allows at least one class.
All inputs are finite; a program needn't handle non-finite values.
Results may differ from a plain program's by a relative error of at most 0.024.
The roundings to bfloat16 on the way count: a program that leaves them out, or rounds other values in their place, can miss the bound.
Values may be sent and summed in bfloat16 or wider, within the bound.
A program may use at most 192 MiB of HBM per device.

v0:
```python
import math

import jax
import jax.numpy as jnp
from jax import lax
from jax.sharding import PartitionSpec as P

ORD = 64
ANG = 128
NAZI = 32
LM = 4096


def copy_for_each(array, axis):
    copies = jnp.broadcast_to(array, (lax.axis_size(axis), *array.shape))
    return lax.all_to_all(copies, axis, split_axis=0, concat_axis=0, tiled=True)


def in_order(blocks, dim):
    shape = list(blocks.shape[1:])
    shape[dim] *= blocks.shape[0]
    return jnp.moveaxis(blocks, 0, dim).reshape(shape)


def gathered_copies(array, axis, dim):
    blocks = copy_for_each(array, axis)
    return in_order(blocks, dim)


def gathered_once(array, axis):
    leaves = jax.tree.leaves(array)
    sequence = sorted(range(len(leaves)), key=lambda k: -leaves[k].size)
    width = (1, *leaves[sequence[0]].shape)[-1]
    lines = [
        jnp.pad(leaves[k].reshape(-1), (0, -leaves[k].size % width)).reshape(-1, width)
        for k in sequence
    ]
    both, at, found = (copy_for_each(jnp.concatenate(lines), axis), 0, {})
    for k, line in zip(sequence, lines):
        slab = both[:, at : at + len(line)].reshape(len(both), -1)
        found[k] = slab[:, : leaves[k].size].reshape(-1, *leaves[k].shape)
        at += len(line)
    numbers = iter(range(len(leaves)))
    return jax.tree.map(lambda _: found[next(numbers)], array)


def combined_pairwise(pieces, combine):
    while len(jax.tree.leaves(pieces)[0]) > 1:
        pieces = jax.vmap(combine)(
            *(jax.tree.map(lambda part: part[side::2], pieces) for side in (0, 1))
        )
    return jax.tree.map(lambda part: part[0], pieces)


def joined_all(array, axis, combine):
    pieces = gathered_once(array, axis)
    return combined_pairwise(pieces, combine)


def in_blocks(array, dim, size):
    shape = array.shape
    blocks = array.reshape(*shape[:dim], size, shape[dim] // size, *shape[dim + 1 :])
    return jnp.moveaxis(blocks, dim, 0)


def summed_on_arrival(array, axis, dim):
    blocks = in_blocks(array, dim, lax.axis_size(axis))
    arrived = lax.all_to_all(blocks, axis, split_axis=0, concat_axis=0, tiled=True)
    return arrived.astype(jnp.float32).sum(axis=0)


def taken_together(array, axis):
    everything = copy_for_each(array, axis)
    return jnp.sum(everything.astype(jnp.float32), axis=0)


def synth_table():
    orders = (jnp.arange(ORD) - ORD // 2).astype(jnp.float32)
    angles = jnp.arange(ANG).astype(jnp.float32) * (2.0 * math.pi / ANG)
    phase = orders[:, None] * angles[None, :]
    cosine = jnp.cos(phase)
    sine = jnp.sin(phase)
    upper = jnp.concatenate([cosine, sine], axis=1)
    lower = jnp.concatenate([-sine, cosine], axis=1)
    return (jnp.concatenate([upper, lower], axis=0) * ORD ** (-0.5)).astype(jnp.bfloat16)


def rotated_ops(tilts, azimuths, slice_ops):
    chosen = jnp.take(slice_ops, tilts, axis=0).astype(jnp.float32)
    chosen = jnp.transpose(chosen, (1, 0, 2))
    orders = (jnp.arange(LM) % ORD - ORD // 2).astype(jnp.float32)
    turns = azimuths.astype(jnp.float32) * (2.0 * math.pi / NAZI)
    phase = orders[:, None] * turns[None, :]
    cosine = jnp.cos(phase)[:, :, None]
    sine = jnp.sin(phase)[:, :, None]
    upper = jnp.concatenate([cosine * chosen, -sine * chosen], axis=2)
    lower = jnp.concatenate([sine * chosen, cosine * chosen], axis=2)
    rotator = jnp.concatenate([upper, lower], axis=0)
    return rotator.reshape(2 * LM, -1).astype(jnp.bfloat16)


def synthesize(coefs, rotator, angle_table):
    classes, radial = (coefs.shape[0], coefs.shape[1])
    flat_coef = coefs.reshape(classes * radial, 2 * LM)
    harmonics = jnp.dot(flat_coef, rotator, preferred_element_type=jnp.float32).astype(jnp.bfloat16)
    orients = rotator.shape[1] // (2 * ORD)
    harmonics = (
        harmonics.reshape(classes, radial, orients, 2 * ORD)
        .transpose(2, 0, 1, 3)
        .reshape(-1, 2 * ORD)
    )
    values = jnp.dot(harmonics, angle_table, preferred_element_type=jnp.float32).astype(
        jnp.bfloat16
    )
    return values


def adjoint(back_proj, rotator, angle_table, radial, classes):
    columns = back_proj.shape[1]
    orients = rotator.shape[1] // (2 * ORD)
    spread = (
        back_proj.reshape(radial, 2 * ANG, columns)
        .transpose(0, 2, 1)
        .reshape(radial * columns, 2 * ANG)
    )
    harmonics = jnp.dot(spread, angle_table.T, preferred_element_type=jnp.float32).astype(
        jnp.bfloat16
    )
    harmonics = harmonics.reshape(radial, orients, classes, 2 * ORD).transpose(2, 0, 1, 3)
    harmonics = harmonics.reshape(classes * radial, orients * 2 * ORD)
    return lax.dot_general(
        harmonics, rotator, (((1,), (1,)), ((), ())), preferred_element_type=jnp.float32
    )


def combine_parts(former, latter):
    row_peak = jnp.maximum(former[0], latter[0])
    totals = (
        former[1] * jnp.exp(former[0] - row_peak)[:, None]
        + latter[1] * jnp.exp(latter[0] - row_peak)[:, None]
    )
    return (row_peak, totals)


def body(
    images,
    ctf_class,
    class_mask,
    precision,
    class_log_prior,
    ctf_filters,
    volume_coef,
    slice_ops,
    tilt_index,
    azimuth_index,
):
    angle_table = synth_table()
    image_rows = images.shape[0]
    classes = volume_coef.shape[0]
    radial = volume_coef.shape[1]
    orients = tilt_index.shape[0]
    filter_count = ctf_filters.shape[0]
    selector = (ctf_class[:, None] == jnp.arange(filter_count)[None, :]).astype(jnp.float32)
    ctf_rows = jnp.dot(selector, ctf_filters, precision=lax.Precision.HIGHEST)
    filtered = (images.astype(jnp.float32) * ctf_rows).astype(jnp.bfloat16)
    ctf_square = ctf_filters * ctf_filters
    rotator = rotated_ops(tilt_index, azimuth_index, slice_ops)
    templates = synthesize(volume_coef, rotator, angle_table)
    segment = gathered_copies(templates, "img", 1)
    part_img = filtered
    correl = lax.dot_general(
        part_img, segment, (((1,), (1,)), ((), ())), preferred_element_type=jnp.float32
    )
    square = segment.astype(jnp.float32)
    square = square * square
    energy = lax.dot_general(
        ctf_square, square, (((1,), (1,)), ((), ())), precision=lax.Precision.HIGHEST
    )
    correl, energy = (correl, energy)
    energy_rows = jnp.dot(selector, energy, precision=lax.Precision.HIGHEST)
    score = precision[:, None] * (correl - 0.5 * energy_rows) + jnp.tile(
        class_log_prior, (1, orients)
    )
    allowed = jnp.tile(class_mask, (1, orients)) > 0
    score = jnp.where(allowed, score, -1e30)
    local_peak = jnp.max(score, axis=1)
    local_totals = (
        jnp.exp(score - local_peak[:, None]).reshape(image_rows, orients, classes).sum(axis=1)
    )
    row_peak, totals = joined_all((local_peak, local_totals), "ori", combine_parts)
    exponent = jnp.exp(score - row_peak[:, None])
    norm_sum = totals.sum(axis=1)
    log_evidence = row_peak + jnp.log(norm_sum)
    class_posterior = totals / norm_sum[:, None]
    weights = (exponent / norm_sum[:, None]).astype(jnp.bfloat16)
    part_img = filtered
    summed = summed_on_arrival(
        lax.dot_general(
            part_img, weights, (((0,), (0,)), ((), ())), preferred_element_type=jnp.float32
        ).astype(jnp.bfloat16),
        "img",
        0,
    ).astype(jnp.bfloat16)
    coef_own = adjoint(summed, rotator, angle_table, radial, classes)
    coef_sum = (
        taken_together(coef_own.astype(jnp.bfloat16), "ori")
        .astype(jnp.float32)
        .reshape(classes, radial, 2, LM)
    )
    return (coef_sum, log_evidence, class_posterior)


def solution(mesh):
    placed = (
        P("img", None),
        P("img"),
        P("img", None),
        P("img"),
        P("img", None),
        P(),
        P(None, "img", None, None),
        P(),
        P("ori"),
        P("ori"),
    )
    return jax.shard_map(
        body,
        mesh=mesh,
        in_specs=placed,
        out_specs=(P(None, "img", None, None), P("img"), P("img", None)),
        check_vma=False,
    )
```

profile of v0, /device:TPU:2, one launch (start us, length us, event | category | flops | bytes accessed | tf_op | source)
XLA Modules:
  0.0 216.7 jit_solution(13650449595834580542)
XLA Ops:
  0.6 0.7 compare_select_fusion
  1.3 0.7 compare_and_fusion
  2.0 0.7 convert_multiply_fusion.1
  2.6 1.0 copy.49
  3.6 1.0 fusion.22
  4.6 6.9 %gather_fusion = bf16[16,4096,64]{1,2,0:T(8,128)(2,1)} fusion(bf16[8,4096,64]{1,2,0:T(8,128)(2,1)} %param.17, s32[1024]{0:T(1024)S(1)} %pad_clamp_fusion), kind=kCustom, calls=%fused_computation | custom fusion | bytes 16777280 | tf_op jit(solution)/shard_map/jit(_take)/gather | solution.py:89
  11.5 0.2 multiply_sine_fusion.1
  11.7 11.7 %fusion.3 = (bf16[4096,16,64]{0,2,1:T(8,128)(2,1)}, bf16[4096,16,64]{0,2,1:T(8,128)(2,1)}, bf16[4096,16,64]{0,2,1:T(8,128)(2,1)}) fusion(f32[4096,16]{0,1:T(8,128)S(1)} %get-tuple-element.22, bf16[16,4096,64]{1,2,0:T(8,128)(2,1)} %gather_fusion, pred[16]{0:T(512)(128)(4,1)S(1)} %compare_and_fusion, f32[4096,16]{0,1:T(8,128)S(1)} %get-tuple-element.23, ...), kind=kLoop, calls=%fused_computation.10 | loop fusion | flops 33554432 | bytes 34340880 | tf_op jit(solution)/shard_map/convert.9
  23.5 25.1 %pad_maximum_fusion.3 = (bf16[4096,16,128]{0,2,1:T(8,128)(2,1)}, bf16[4096,16,128]{0,2,1:T(8,128)(2,1)}) fusion(bf16[4096,16,64]{0,2,1:T(8,128)(2,1)} %get-tuple-element.17, bf16[4096,16,64]{0,2,1:T(8,128)(2,1)} %get-tuple-element.19, bf16[4096,16,64]{0,2,1:T(8,128)(2,1)} %get-tuple-element.18), kind=kLoop, calls=%fused_computation.4 | loop fusion | flops 67108864 | bytes 58720256 | tf_op jit(solution)/shard_map/concatenate | solution.py:96
  48.6 14.1 %fusion.15 = bf16[128,128]{1,0:T(8,128)(2,1)S(1)} fusion(bf16[8,8192]{1,0:T(8,128)(2,1)S(1)} %bitcast.74, bf16[4096,2048]{0,1:T(8,128)(2,1)} %bitcast.65, bf16[4096,2048]{0,1:T(8,128)(2,1)} %bitcast.63), kind=kOutput, calls=%fused_computation.29 | convolution fusion | flops 335560704 | bytes 33718272 | tf_op jit(solution)/shard_map/dot_general | solution.py:105
  62.9 1.2 broadcast_in_dim.25
  64.1 6.1 %all-to-all-start = ((bf16[16,128,256]{1,2,0:T(8,128)(2,1)}), bf16[16,128,256]{1,2,0:T(8,128)(2,1)S(1)}, u32[]{:S(2)}, u32[]{:S(2)}) async-start(bf16[16,128,256]{1,2,0:T(8,128)(2,1)} %broadcast_in_dim.25), calls=%async_computation | async-start | bytes 2097152 | tf_op jit(solution)/shard_map/all_to_all | solution.py:16
  70.3 6.9 %multiply_convert_fusion = bf16[512,4096]{1,0:T(8,128)(2,1)} fusion(bf16[512,4096]{1,0:T(8,128)(2,1)} %param.10, f32[16,4096]{1,0:T(8,128)S(1)} %copy-done, s32[512]{0:T(512)S(1)} %copy-done.3), kind=kOutput, calls=%fused_computation.13 | convolution fusion | flops 408952832 | bytes 8652800 | tf_op jit(solution)/shard_map/dot_general | solution.py:164
  77.2 11.1 %all-to-all-done = bf16[16,128,256]{1,2,0:T(8,128)(2,1)S(1)} async-done(((bf16[16,128,256]{1,2,0:T(8,128)(2,1)}), bf16[16,128,256]{1,2,0:T(8,128)(2,1)S(1)}, u32[]{:S(2)}, u32[]{:S(2)}) %all-to-all-start) | async-done | bytes 1048608 | tf_op jit(solution)/shard_map/all_to_all | solution.py:16
  88.3 1.3 fusion.7
  89.6 3.7 %fusion.39 = f32[512,128]{0,1:T(8,128)S(1)} fusion(bf16[512,4096]{1,0:T(8,128)(2,1)} %multiply_convert_fusion, bf16[128,4096]{0,1:T(8,128)(2,1)S(1)} %bitcast.68), kind=kOutput, calls=%fused_computation.83 | convolution fusion | flops 536870912 | bytes 5505024 | tf_op jit(solution)/shard_map/dot_general | solution.py:171
  93.3 0.4 fusion.38
  94.0 21.4 %all_to_all.20 = f32[16,576,8]{1,2,0:T(8,128)S(1)} all-to-all(f32[16,576,8]{1,2,0:T(8,128)S(1)} %broadcast_in_dim.27), channel_id=1, replica_groups=mesh['img'=16,'ori'=16] {'ori'}, dimensions={0} | all-to-all | bytes 589824 | tf_op jit(solution)/shard_map/all_to_all | solution.py:16
  115.4 0.2 copy.43
  115.6 1.1 slice.59
  116.7 1.2 slice.60
  118.4 3.5 %convolution_convert_fusion = bf16[4096,128]{1,0:T(8,128)(2,1)S(1)} fusion(bf16[512,4096]{1,0:T(8,128)(2,1)} %multiply_convert_fusion, f32[512,128]{0,1:T(8,128)S(1)} %get-tuple-element.29, f32[512]{0:T(512)S(1)} %fusion.32, f32[512]{0:T(512)S(1)} %bitcast.79), kind=kOutput, calls=%fused_computation.15 | convolution fusion | flops 537591808 | bytes 5509120 | tf_op jit(solution)/shard_map/dot_general | solution.py:198
  122.0 21.0 %all_to_all.21 = bf16[16,256,128]{2,1,0:T(8,128)(2,1)S(1)} all-to-all(bf16[16,256,128]{2,1,0:T(8,128)(2,1)S(1)} %bitcast.72), channel_id=1, replica_groups=mesh['img'=16,'ori'=16] {'img'}, dimensions={0} | all-to-all | bytes 2097152 | tf_op jit(solution)/shard_map/all_to_all | solution.py:68
  143.0 0.1 reduce_sum.41
  143.1 16.2 %fusion.5 = bf16[8,8192]{1,0:T(8,128)(2,1)S(1)} fusion(bf16[4096,2048]{0,1:T(8,128)(2,1)} %bitcast.66, bf16[4096,2048]{0,1:T(8,128)(2,1)} %bitcast.64, bf16[256,128]{1,0:T(8,128)(2,1)S(1)} %reduce_sum.41, f32[64,128]{1,0:T(8,128)S(1)} %get-tuple-element.27, f32[64,128]{1,0:T(8,128)S(1)} %get-tuple-element.26, f32[64,128]{1,0:T(8,128)S(1)} %get-tuple-element.25), kind=kOutput, calls=%fused_computation.12 | convolution fusion | flops 344178688 | bytes 33849344 | tf_op jit(solution)/shard_map/dot_general | solution.py:131
  159.3 1.5 broadcast_in_dim.28
  160.8 5.6 %all-to-all-start.3 = ((bf16[16,8,8192]{2,1,0:T(8,128)(2,1)}), bf16[16,8,8192]{2,1,0:T(8,128)(2,1)S(1)}, u32[]{:S(2)}, u32[]{:S(2)}) async-start(bf16[16,8,8192]{2,1,0:T(8,128)(2,1)} %broadcast_in_dim.28), calls=%async_computation.3 | async-start | bytes 4194304 | tf_op jit(solution)/shard_map/all_to_all | solution.py:16
  166.4 0.6 log_add_fusion
  167.0 0.6 bitcast_divide_fusion
  167.6 47.9 %all-to-all-done.3 = bf16[16,8,8192]{2,1,0:T(8,128)(2,1)S(1)} async-done(((bf16[16,8,8192]{2,1,0:T(8,128)(2,1)}), bf16[16,8,8192]{2,1,0:T(8,128)(2,1)S(1)}, u32[]{:S(2)}, u32[]{:S(2)}) %all-to-all-start.3) | async-done | bytes 2097184 | tf_op jit(solution)/shard_map/all_to_all | solution.py:16
  215.5 0.3 convert_reduce_fusion
  215.8 0.9 copy.46
  (42 shorter events, 1.1 us)
Async XLA Ops:
  48.6 21.7 %copy-start.2 = (s32[512,8]{0,1:T(8,128)S(1)}, s32[512,8]{0,1:T(8,128)}, u32[]{:S(2)}) copy-start(s32[512,8]{0,1:T(8,128)} %param.12) | copy-start | bytes 49156
  48.6 21.7 %copy-start = (f32[16,4096]{1,0:T(8,128)S(1)}, f32[16,4096]{1,0:T(8,128)}, u32[]{:S(2)}) copy-start(f32[16,4096]{1,0:T(8,128)} %param.15) | copy-start | bytes 786436
  48.6 21.7 %copy-start.3 = (s32[512]{0:T(512)S(1)}, s32[512]{0:T(512)}, u32[]{:S(2)}) copy-start(s32[512]{0:T(512)} %param.11) | copy-start | bytes 6148
  62.6 30.7 %copy-start.1 = (f32[512,8]{0,1:T(8,128)S(1)}, f32[512,8]{0,1:T(8,128)}, u32[]{:S(2)}) copy-start(f32[512,8]{0,1:T(8,128)} %param.14) | copy-start | bytes 49156
  62.7 30.7 %copy-start.4 = (f32[512]{0:T(512)S(1)}, f32[512]{0:T(512)}, u32[]{:S(2)}) copy-start(f32[512]{0:T(512)} %param.13) | copy-start | bytes 6148
  64.1 24.2 %all-to-all-start = ((bf16[16,128,256]{1,2,0:T(8,128)(2,1)}), bf16[16,128,256]{1,2,0:T(8,128)(2,1)S(1)}, u32[]{:S(2)}, u32[]{:S(2)}) async-start(bf16[16,128,256]{1,2,0:T(8,128)(2,1)} %broadcast_in_dim.25), calls=%async_computation | async-start | bytes 2097152 | tf_op jit(solution)/shard_map/all_to_all | solution.py:16
  160.8 54.6 %all-to-all-start.3 = ((bf16[16,8,8192]{2,1,0:T(8,128)(2,1)}), bf16[16,8,8192]{2,1,0:T(8,128)(2,1)S(1)}, u32[]{:S(2)}, u32[]{:S(2)}) async-start(bf16[16,8,8192]{2,1,0:T(8,128)(2,1)} %broadcast_in_dim.28), calls=%async_computation.3 | async-start | bytes 4194304 | tf_op jit(solution)/shard_map/all_to_all | solution.py:16
where the time goes:
time: 217 us
  waiting for transfers between devices  59 us (27%)
  matrix products  46.2 us (21%)
  blocking collectives  42.4 us (20%)
  other arithmetic  41.9 us (19%)
  local copies, waits for them, and re-layouts  14.6 us (7%)
  starting transfers between devices  11.7 us (5%)
    all_to_all x2, waiting for transfers between devices, copy_for_each(): return lax.all_to_all(copies, axis, split_axis=0, concat_axis=0, tiled=True)  59 us
    concatenate x1, other arithmetic, rotated_ops(): upper = jnp.concatenate([cosine * chosen, -sine * chosen], axis=2)  25.1 us
    all_to_all x1, blocking collectives, copy_for_each(): return lax.all_to_all(copies, axis, split_axis=0, concat_axis=0, tiled=True)  21.4 us
    all_to_all x1, blocking collectives, summed_on_arrival(): lax.all_to_all(blocks, axis, split_axis=0, concat_axis=0, tiled=True)  21 us
    dot_general x1, matrix products, adjoint(): lax.dot_general(harmonics, rotator, (((1,), (1,)), ((), ())), preferred_e...  16.2 us
    dot_general x1, matrix products, synthesize(): jnp.dot(flat_coef, rotator, preferred_element_type=jnp.float32)  14.1 us
    another operation x1, other arithmetic  11.7 us
    all_to_all x2, starting transfers between devices, copy_for_each(): return lax.all_to_all(copies, axis, split_axis=0, concat_axis=0, tiled=True)  11.7 us
  transfers between devices with their start and end apart: 2, of which 2 were waited for; matrix products, arithmetic and copies ran while one was open for 4% of the time, Pallas kernels for 0%

commit v1 on v0

v1 whole, which is shorter than its diff:
```python
import functools
import math

import jax
import jax.numpy as jnp
import numpy as np
from jax import lax
from jax.experimental import pallas as pl
from jax.experimental.pallas import tpu as pltpu
from jax.sharding import PartitionSpec as P

ORD = 64
ANG = 128
NAZI = 32
F32 = jnp.float32
BF16 = jnp.bfloat16
MESH = pl.DeviceIdType.MESH
NT = (((1,), (1,)), ((), ()))
NN = (((1,), (0,)), ((), ()))


def angle_table():
    orders = np.arange(ORD) - ORD // 2
    phase = orders[:, None] * np.arange(ANG)[None, :] * (2.0 * math.pi / ANG)
    upper = np.concatenate([np.cos(phase), np.sin(phase)], axis=1)
    lower = np.concatenate([-np.sin(phase), np.cos(phase)], axis=1)
    table = np.concatenate([upper, lower], axis=0) * ORD**-0.5
    return jnp.asarray(table.astype(np.float32)).astype(BF16)


def azimuth_table():
    orders = np.arange(2 * ORD) % ORD - ORD // 2
    phase = np.arange(NAZI)[:, None] * orders[None, :] * (2.0 * math.pi / NAZI)
    table = np.concatenate([np.cos(phase), np.sin(phase)], axis=1)
    return jnp.asarray(table.astype(np.float32))


def dot(a, b, dims, precision=None):
    return lax.dot_general(a, b, dims, precision=precision, preferred_element_type=F32)


def kernel(
    n_img,
    n_ori,
    images,
    cls_ref,
    mask_ref,
    prec_ref,
    prior_ref,
    ctf_ref,
    vol_ref,
    slices,
    tilt_ref,
    azi_ref,
    turn_ref,
    ang_ref,
    coef_ref,
    logev_ref,
    post_ref,
    img_v,
    s_v,
    x_v,
    fa_v,
    turns,
    chl,
    hbuf,
    lbuf,
    pbuf,
    hs,
    hr,
    cs,
    cr,
    cfin,
    local_sem,
    send_sem,
    recv_sem,
):
    me_a = lax.axis_index("img")
    me_o = lax.axis_index("ori")
    classes = vol_ref.shape[0]
    lm = vol_ref.shape[2]
    orients = tilt_ref.shape[0]
    rows = orients * classes
    n_images = cls_ref.shape[1]
    nctf = ctf_ref.shape[0]
    span = s_v.shape[0]
    chunk = lm // n_ori

    def partner(me, step, n):
        return lax.rem(me + step, n)

    def put(phase, src, dst, axis, other, send_slot, recv_slot):
        return pltpu.make_async_remote_copy(
            src_ref=src,
            dst_ref=dst,
            send_sem=send_sem.at[phase, send_slot],
            recv_sem=recv_sem.at[phase, recv_slot],
            device_id={axis: other},
            device_id_type=MESH,
        )

    fetch_s = pltpu.make_async_copy(slices, s_v, local_sem.at[0])
    fetch_s.start()
    fetch_i = pltpu.make_async_copy(images, img_v, local_sem.at[1])
    fetch_i.start()

    barrier = pltpu.get_barrier_semaphore()

    def greet(axis, me, n):
        def one(step, carry):
            pl.semaphore_signal(
                barrier, inc=1, device_id={axis: partner(me, step, n)}, device_id_type=MESH
            )
            return carry

        lax.fori_loop(1, n, one, 0)

    greet("img", me_a, n_img)
    greet("ori", me_o, n_ori)

    v_re = vol_ref[:, 0, :].astype(F32)
    v_im = vol_ref[:, 1, :].astype(F32)

    def rotate(o, carry):
        turn = turn_ref[pl.ds(azi_ref[o], 1), :]
        cos8 = jnp.broadcast_to(turn[:, :ANG], (classes, ANG))
        sin8 = jnp.broadcast_to(turn[:, ANG:], (classes, ANG))
        turns[o, 0] = cos8
        turns[o, 1] = sin8
        for j in range(lm // ANG):
            cols = slice(j * ANG, (j + 1) * ANG)
            re, im = v_re[:, cols], v_im[:, cols]
            both = jnp.concatenate([re * cos8 + im * sin8, im * cos8 - re * sin8], axis=0)
            x_v[pl.ds(pl.multiple_of(o * 16, 16), 16), cols] = both.astype(BF16)
        return carry

    lax.fori_loop(0, orients, rotate, 0)

    fetch_s.wait()
    spread = dot(x_v[...], s_v[...], NT).reshape(orients, 2, classes, span)
    lane = lax.broadcasted_iota(jnp.int32, (classes, span), 1) // ORD
    low = lax.broadcasted_iota(jnp.int32, (classes, 2 * ORD), 1) < ORD
    parts = []
    for o in range(orients):
        chosen = lane == tilt_ref[o]
        halves = []
        for c in range(2):
            kept = jnp.where(chosen, spread[o, c], 0.0)
            fold = kept[:, : 2 * ORD]
            for b in range(1, span // (2 * ORD)):
                fold = fold + kept[:, b * 2 * ORD : (b + 1) * 2 * ORD]
            halves.append(fold + pltpu.roll(fold, ORD, 1))
        parts.append(jnp.where(low, halves[0], halves[1]))
    harm = jnp.concatenate(parts, axis=0).astype(BF16)
    ang = ang_ref[...]
    temp = dot(harm, ang, NN).astype(BF16).astype(F32)
    own = pl.ds(pl.multiple_of(me_a * 2 * ANG, 2 * ANG), 2 * ANG)
    ctf_own = ctf_ref[:, own]
    energy_own = dot(ctf_own * ctf_own, temp * temp, NT, lax.Precision.HIGHEST)
    e_hi = energy_own.astype(BF16)
    e_lo = (energy_own - e_hi.astype(F32)).astype(BF16)
    hbuf[me_a, 0:rows, :] = harm
    hbuf[me_a, rows : rows + nctf, :] = e_hi
    hbuf[me_a, rows + nctf : rows + 2 * nctf, :] = e_lo

    pl.semaphore_wait(barrier, n_img - 1 + n_ori - 1)

    def send_harm(step, carry):
        to = partner(me_a, step, n_img)
        put(0, hbuf.at[me_a], hbuf.at[me_a], "img", to, step, me_a).start()
        return carry

    lax.fori_loop(1, n_img, send_harm, 0)

    ctf_hi = ctf_ref[...].astype(BF16)
    chl[0:nctf, :] = ctf_hi
    chl[nctf : 2 * nctf, :] = (ctf_ref[...] - ctf_hi.astype(F32)).astype(BF16)
    cls = cls_ref[...]
    hot2 = lax.rem(lax.broadcasted_iota(jnp.int32, (2 * nctf, n_images), 0), nctf) == cls
    hot2 = jnp.where(hot2, 1.0, 0.0).T.astype(BF16)
    fetch_i.wait()

    def shell(r, carry):
        cols = pl.ds(pl.multiple_of(r * 2 * ANG, 2 * ANG), 2 * ANG)
        ctf_rows = dot(hot2, chl[:, cols], NN)
        filtered = (img_v[:, cols].astype(F32) * ctf_rows).astype(BF16)
        proj = dot(filtered, ang, NT).astype(BF16)
        fa_v[:, pl.ds(pl.multiple_of(r * 2 * ORD, 2 * ORD), 2 * ORD)] = proj
        return carry

    lax.fori_loop(0, n_img, shell, 0)

    def take_harm(step, carry):
        sender = partner(me_a, step, n_img)
        put(0, hbuf.at[sender], hbuf.at[sender], "img", sender, step, sender).wait_recv()
        return carry

    lax.fori_loop(1, n_img, take_harm, 0)
    all_harm = jnp.concatenate([hbuf[r, 0:rows, :] for r in range(n_img)], axis=1)
    correl = dot(all_harm, fa_v[...], NT)
    energy = jnp.zeros((nctf, rows), F32)
    for r in range(n_img):
        energy = energy + hbuf[r, rows : rows + nctf, :].astype(F32)
        energy = energy + hbuf[r, rows + nctf : rows + 2 * nctf, :].astype(F32)
    hot = jnp.where(lax.broadcasted_iota(jnp.int32, (nctf, n_images), 0) == cls, 1.0, 0.0)
    energy_rows = dot(energy.T, hot, NN, lax.Precision.HIGHEST)
    score = prec_ref[...] * (correl - 0.5 * energy_rows)
    score = score.reshape(orients, classes, n_images) + prior_ref[...][None]
    score = jnp.where((mask_ref[...] > 0)[None], score, -1e30)
    peak = jnp.max(jnp.max(score, axis=0), axis=0, keepdims=True)
    exponent = jnp.exp(score - peak[None])
    totals = jnp.sum(exponent, axis=0)
    local_lse = peak + jnp.log(jnp.sum(totals, axis=0, keepdims=True))
    lbuf[me_o] = local_lse

    def send_lse(step, carry):
        to = partner(me_o, step, n_ori)
        put(1, lbuf.at[me_o], lbuf.at[me_o], "ori", to, step, me_o).start()
        return carry

    lax.fori_loop(1, n_ori, send_lse, 0)

    def take_lse(step, carry):
        sender = partner(me_o, step, n_ori)
        put(1, lbuf.at[sender], lbuf.at[sender], "ori", sender, step, sender).wait_recv()
        return carry

    lax.fori_loop(1, n_ori, take_lse, 0)
    all_lse = lbuf[...]
    top = jnp.max(all_lse, axis=0)
    lse = top + jnp.log(jnp.sum(jnp.exp(all_lse - top[None]), axis=0))
    logev_ref[...] = lse
    scale = jnp.exp(peak - lse)
    weights = (exponent * scale[None]).reshape(rows, n_images).astype(BF16)

    def back(step, carry):
        to = partner(me_a, step, n_img)
        cols = pl.ds(pl.multiple_of(to * 2 * ORD, 2 * ORD), 2 * ORD)
        hs[to] = dot(weights, fa_v[:, cols], NN).astype(BF16)

        @pl.when(step < n_img)
        def _():
            put(2, hs.at[to], hr.at[me_a], "img", to, step, me_a).start()

        return carry

    lax.fori_loop(1, n_img + 1, back, 0)

    share = totals * scale
    half = n_images // 2
    share = jnp.concatenate([share[:, :half], share[:, half:]], axis=0)
    pbuf[me_o] = share.astype(BF16)

    def send_share(step, carry):
        to = partner(me_o, step, n_ori)
        put(3, pbuf.at[me_o], pbuf.at[me_o], "ori", to, step, me_o).start()
        return carry

    lax.fori_loop(1, n_ori, send_share, 0)

    def take_back(step, total):
        sender = partner(me_a, step, n_img)
        put(2, hs.at[sender], hr.at[sender], "img", sender, step, sender).wait_recv()
        return total + hr[sender].astype(F32)

    summed = lax.fori_loop(1, n_img, take_back, hs[me_a].astype(F32))
    summed = summed.astype(BF16).astype(F32)

    blocks = []
    for o in range(orients):
        piece = summed[o * classes : (o + 1) * classes, :]
        turned = pltpu.roll(piece, ORD, 1)
        chosen = lane == tilt_ref[o]
        for both in (jnp.where(low, piece, turned), jnp.where(low, turned, piece)):
            wide = jnp.concatenate([both] * (span // (2 * ORD)), axis=1)
            blocks.append(jnp.where(chosen, wide, 0.0))
    placed = jnp.concatenate(blocks, axis=0).astype(BF16)
    cos_all = jnp.concatenate([turns[:, 0]] * (chunk // ANG), axis=2)
    sin_all = jnp.concatenate([turns[:, 1]] * (chunk // ANG), axis=2)

    def coef(step, carry):
        to = partner(me_o, step, n_ori)
        cols = pl.ds(pl.multiple_of(to * chunk, chunk), chunk)
        wide = dot(placed, s_v[:, cols], NN).reshape(orients, 2, classes, chunk)
        re, im = wide[:, 0], wide[:, 1]
        out_re = jnp.sum(re * cos_all - im * sin_all, axis=0)
        out_im = jnp.sum(re * sin_all + im * cos_all, axis=0)
        cs[to] = jnp.concatenate([out_re, out_im], axis=0).astype(BF16)

        @pl.when(step < n_ori)
        def _():
            put(4, cs.at[to], cr.at[me_o], "ori", to, step, me_o).start()

        return carry

    lax.fori_loop(1, n_ori + 1, coef, 0)

    def take_coef(step, total):
        sender = partner(me_o, step, n_ori)
        put(4, cs.at[sender], cr.at[sender], "ori", sender, step, sender).wait_recv()
        return total + cr[sender].astype(F32)

    total = lax.fori_loop(1, n_ori, take_coef, cs[me_o].astype(F32))
    cfin[me_o] = total.astype(BF16)

    def send_final(step, carry):
        to = partner(me_o, step, n_ori)
        put(5, cfin.at[me_o], cfin.at[me_o], "ori", to, step, me_o).start()
        return carry

    lax.fori_loop(1, n_ori, send_final, 0)

    def take_share(step, total):
        sender = partner(me_o, step, n_ori)
        put(3, pbuf.at[sender], pbuf.at[sender], "ori", sender, step, sender).wait_recv()
        return total + pbuf[sender].astype(F32)

    share = lax.fori_loop(1, n_ori, take_share, share)
    post_ref[...] = jnp.concatenate([share[:classes], share[classes:]], axis=1)

    def take_final(step, carry):
        sender = partner(me_o, step, n_ori)
        put(5, cfin.at[sender], cfin.at[sender], "ori", sender, step, sender).wait_recv()
        return carry

    lax.fori_loop(1, n_ori, take_final, 0)
    for j in range(n_ori):
        coef_ref[:, j * chunk : (j + 1) * chunk] = cfin[j].astype(F32)

    def drain(step, carry):
        to = partner(me_a, step, n_img)
        put(0, hbuf.at[me_a], hbuf.at[me_a], "img", to, step, me_a).wait_send()
        put(2, hs.at[to], hr.at[me_a], "img", to, step, me_a).wait_send()
        return carry

    lax.fori_loop(1, n_img, drain, 0)

    def drain_ori(step, carry):
        to = partner(me_o, step, n_ori)
        put(1, lbuf.at[me_o], lbuf.at[me_o], "ori", to, step, me_o).wait_send()
        put(3, pbuf.at[me_o], pbuf.at[me_o], "ori", to, step, me_o).wait_send()
        put(4, cs.at[to], cr.at[me_o], "ori", to, step, me_o).wait_send()
        put(5, cfin.at[me_o], cfin.at[me_o], "ori", to, step, me_o).wait_send()
        return carry

    lax.fori_loop(1, n_ori, drain_ori, 0)


def body(
    n_img,
    n_ori,
    images,
    ctf_class,
    class_mask,
    precision,
    class_log_prior,
    ctf_filters,
    volume_coef,
    slice_ops,
    tilt_index,
    azimuth_index,
):
    n_images, size = images.shape
    classes, lm = volume_coef.shape[0], volume_coef.shape[3]
    tilts = slice_ops.shape[0]
    orients = tilt_index.shape[0]
    nctf = ctf_filters.shape[0]
    rows = orients * classes
    span = tilts * ORD
    chunk = lm // n_ori
    slots = max(n_img, n_ori)
    vmem = pl.BlockSpec(memory_space=pltpu.VMEM)
    smem = pl.BlockSpec(memory_space=pltpu.SMEM)
    anywhere = pl.BlockSpec(memory_space=pl.ANY)
    coef, logev, post = pl.pallas_call(
        functools.partial(kernel, n_img, n_ori),
        out_shape=(
            jax.ShapeDtypeStruct((2 * classes, lm), F32),
            jax.ShapeDtypeStruct((1, n_images), F32),
            jax.ShapeDtypeStruct((classes, n_images), F32),
        ),
        in_specs=[anywhere, vmem, vmem, vmem, vmem, vmem, vmem, anywhere, smem, smem, vmem, vmem],
        out_specs=(vmem, vmem, vmem),
        scratch_shapes=[
            pltpu.VMEM((n_images, size), BF16),
            pltpu.VMEM((span, lm), BF16),
            pltpu.VMEM((2 * rows, lm), BF16),
            pltpu.VMEM((n_images, n_img * 2 * ORD), BF16),
            pltpu.VMEM((orients, 2, classes, ANG), F32),
            pltpu.VMEM((2 * nctf, size), BF16),
            pltpu.VMEM((n_img, rows + 2 * nctf, 2 * ORD), BF16),
            pltpu.VMEM((n_ori, 1, n_images), F32),
            pltpu.VMEM((n_ori, 2 * classes, n_images // 2), BF16),
            pltpu.VMEM((n_img, rows, 2 * ORD), BF16),
            pltpu.VMEM((n_img, rows, 2 * ORD), BF16),
            pltpu.VMEM((n_ori, 2 * classes, chunk), BF16),
            pltpu.VMEM((n_ori, 2 * classes, chunk), BF16),
            pltpu.VMEM((n_ori, 2 * classes, chunk), BF16),
            pltpu.SemaphoreType.DMA((2,)),
            pltpu.SemaphoreType.DMA((6, slots)),
            pltpu.SemaphoreType.DMA((6, slots)),
        ],
        compiler_params=pltpu.CompilerParams(
            collective_id=0, has_side_effects=True, vmem_limit_bytes=50 * 2**20
        ),
        cost_estimate=pl.CostEstimate(
            flops=4 * 10**9, bytes_accessed=10**7, transcendentals=10**5
        ),
    )(
        images,
        ctf_class.reshape(1, n_images),
        class_mask.T,
        precision.reshape(1, n_images),
        class_log_prior.T,
        ctf_filters,
        volume_coef.reshape(classes, 2, lm),
        slice_ops.transpose(0, 2, 1).reshape(span, lm),
        tilt_index,
        azimuth_index,
        azimuth_table(),
        angle_table(),
    )
    coef_sum = coef.reshape(2, classes, 1, lm).transpose(1, 2, 0, 3)
    return coef_sum, logev.reshape(n_images), post.T


def solution(mesh):
    placed = (
        P("img", None),
        P("img"),
        P("img", None),
        P("img"),
        P("img", None),
        P(),
        P(None, "img", None, None),
        P(),
        P("ori"),
        P("ori"),
    )
    return jax.shard_map(
        functools.partial(body, mesh.shape["img"], mesh.shape["ori"]),
        mesh=mesh,
        in_specs=placed,
        out_specs=(P(None, "img", None, None), P("img"), P("img", None)),
        check_vma=False,
    )
```

time: 217 us -> 63.2 us (0.29)
  waiting for transfers between devices: 59 us -> 0 us
  Pallas kernels: 0 us -> 52.2 us
  matrix products: 46.2 us -> 0 us
  blocking collectives: 42.4 us -> 0 us
  other arithmetic: 41.9 us -> 0 us
  starting transfers between devices: 11.7 us -> 0 us
  local copies, waits for them, and re-layouts: 14.6 us -> 9.64 us
    all_to_all x2 -> x0, waiting for transfers between devices: 59 us -> none  [copy_for_each(): return lax.all_to_all(copies, axis, split_axis=0, concat_axis=0, tiled=True)]
    pallas_call x0 -> x1, Pallas kernels: none -> 52.2 us  [body(): pl.pallas_call(functools.partial(kernel, n_img, n_ori), out_shape=(jax.Sh...]
    dot_general x8 -> x0, matrix products: 46.2 us -> none  [the longest x1 16.2 us: adjoint(): lax.dot_general(harmonics, rotator, (((1,), (1,)), ((), ())), preferred_e...]
    all_to_all x2 -> x0, blocking collectives: 42.4 us -> none  [the longest x1 21.4 us: copy_for_each(): return lax.all_to_all(copies, axis, split_axis=0, concat_axis=0, tiled=True)]
    concatenate x2 -> x0, other arithmetic: 25.1 us -> none  [the longest x1 25.1 us: rotated_ops(): upper = jnp.concatenate([cosine * chosen, -sine * chosen], axis=2)]
    another operation x1 -> x0, other arithmetic: 11.7 us -> none
    all_to_all x2 -> x0, starting transfers between devices: 11.7 us -> none  [copy_for_each(): return lax.all_to_all(copies, axis, split_axis=0, concat_axis=0, tiled=True)]
    gather x1 -> x0, local copies, waits for them, and re-layouts: 6.92 us -> none  [rotated_ops(): chosen = jnp.take(slice_ops, tilts, axis=0).astype(jnp.float32)]
  transfers between devices with their start and end apart: 2 -> 0, of which waited for: 2 -> 0; matrix products, arithmetic and copies ran while one was open for 4% -> 0% of each run, Pallas kernels for 0% -> 0%
where the time goes in v1:
time: 63.2 us; the launch traced here: 62.5 us
  Pallas kernels  52.2 us (83%)
  local copies, waits for them, and re-layouts  9.64 us (15%)
  between operations  0.66 us (1%)
    pallas_call x1, Pallas kernels, body(): pl.pallas_call(functools.partial(kernel, n_img, n_ori), out_shape=(jax.Sh...  52.2 us
    unnamed x22, local copies, waits for them, and re-layouts  8.73 us

profile of v1, /device:TPU:2, one launch (start us, length us, event | category | flops | bytes accessed | tf_op | source)
XLA Modules:
  0.0 62.5 jit_solution(14188160650346958077)
XLA Ops:
  0.6 0.0 copy-start
  0.6 0.9 %copy-done = f32[16,4096]{1,0:T(8,128)S(1)} copy-done((f32[16,4096]{1,0:T(8,128)S(1)}, f32[16,4096]{1,0:T(8,128)}, u32[]{:S(2)}) %copy-start) | copy-done | bytes 262168
  1.6 0.0 copy-start.1
  1.6 0.9 %copy-done.1 = bf16[8,1,2,4096]{3,2,1,0:T(2,128)(2,1)S(1)} copy-done((bf16[8,1,2,4096]{3,2,1,0:T(2,128)(2,1)S(1)}, bf16[8,1,2,4096]{3,2,1,0:T(2,128)(2,1)}, u32[]{:S(2)}) %copy-start.1) | copy-done | bytes 131096
  2.5 0.0 copy-start.2
  2.5 0.7 %copy-done.2 = s32[512,8]{0,1:T(8,128)S(1)} copy-done((s32[512,8]{0,1:T(8,128)S(1)}, s32[512,8]{0,1:T(8,128)}, u32[]{:S(2)}) %copy-start.2) | copy-done | bytes 16408
  3.2 0.0 copy-start.3
  3.2 0.7 %copy-done.3 = f32[512,8]{0,1:T(8,128)S(1)} copy-done((f32[512,8]{0,1:T(8,128)S(1)}, f32[512,8]{0,1:T(8,128)}, u32[]{:S(2)}) %copy-start.3) | copy-done | bytes 16408
  3.9 0.0 copy-start.4
  3.9 0.7 %copy-done.4 = s32[512]{0:T(512)S(1)} copy-done((s32[512]{0:T(512)S(1)}, s32[512]{0:T(512)}, u32[]{:S(2)}) %copy-start.4) | copy-done | bytes 2072
  4.6 0.0 copy-start.5
  4.6 0.7 %copy-done.5 = f32[512]{0:T(512)S(1)} copy-done((f32[512]{0:T(512)S(1)}, f32[512]{0:T(512)}, u32[]{:S(2)}) %copy-start.5) | copy-done | bytes 2072
  5.3 0.0 copy-start.6
  5.3 0.7 %copy-done.6 = s32[16]{0:T(128)S(1)} copy-done((s32[16]{0:T(128)S(1)}, s32[16]{0:T(128)}, u32[]{:S(2)}) %copy-start.6) | copy-done | bytes 88
  5.9 0.0 copy-start.7
  5.9 0.7 %copy-done.7 = s32[16]{0:T(128)S(1)} copy-done((s32[16]{0:T(128)S(1)}, s32[16]{0:T(128)}, u32[]{:S(2)}) %copy-start.7) | copy-done | bytes 88
  6.6 0.0 copy-start.8
  6.6 0.8 %copy-done.8 = bf16[128,256]{1,0:T(8,128)(2,1)S(1)} copy-done((bf16[128,256]{1,0:T(8,128)(2,1)S(1)}, bf16[128,256]{1,0:T(8,128)(2,1)}, u32[]{:S(2)}) %copy-start.8) | copy-done | bytes 65560
  7.4 0.0 copy-start.9
  7.4 0.8 %copy-done.9 = f32[32,256]{1,0:T(8,128)S(1)} copy-done((f32[32,256]{1,0:T(8,128)S(1)}, f32[32,256]{1,0:T(8,128)}, u32[]{:S(2)}) %copy-start.9) | copy-done | bytes 32792
  8.2 52.2 %shard_map.139 = (f32[16,4096]{1,0:T(8,128)S(1)}, f32[1,512]{1,0:T(1,128)S(1)}, f32[8,512]{1,0:T(8,128)S(1)}) custom-call(bf16[512,4096]{1,0:T(8,128)(2,1)} %images.1, s32[1,512]{1,0:T(1,128)S(1)} %bitcast.20, s32[8,512]{1,0:T(8,128)S(1)} %bitcast.18, f32[1,512]{1,0:T(1,128)S(1)} %bitcast.21, f32[8,512]{1,0:T(8,128)S(1)} %bitcast.19, ...), custom_call_target="tpu_custom_call" | custom-call | flops 4000000000 | bytes 10000000 | tf_op jit(solution)/shard_map/pallas_call | solution.py:375
  60.4 0.9 %copy.17 = f32[2,8,1,4096]{3,0,2,1:T(2,128)} copy(f32[2,8,1,4096]{3,1,0,2:T(8,128)S(1)} %bitcast.14) | data formatting | bytes 524288 | tf_op jit(solution)/shard_map/reshape | solution.py:423
  61.4 0.6 copy.20
  61.9 0.6 copy.21
Async XLA Ops:
  0.6 1.0 %copy-start = (f32[16,4096]{1,0:T(8,128)S(1)}, f32[16,4096]{1,0:T(8,128)}, u32[]{:S(2)}) copy-start(f32[16,4096]{1,0:T(8,128)} %ctf_ref.1) | copy-start | bytes 786436
  1.6 0.9 %copy-start.1 = (bf16[8,1,2,4096]{3,2,1,0:T(2,128)(2,1)S(1)}, bf16[8,1,2,4096]{3,2,1,0:T(2,128)(2,1)}, u32[]{:S(2)}) copy-start(bf16[8,1,2,4096]{3,2,1,0:T(2,128)(2,1)} %param.18) | copy-start | bytes 393220
  2.5 0.7 %copy-start.2 = (s32[512,8]{0,1:T(8,128)S(1)}, s32[512,8]{0,1:T(8,128)}, u32[]{:S(2)}) copy-start(s32[512,8]{0,1:T(8,128)} %param.14) | copy-start | bytes 49156
  3.2 0.7 %copy-start.3 = (f32[512,8]{0,1:T(8,128)S(1)}, f32[512,8]{0,1:T(8,128)}, u32[]{:S(2)}) copy-start(f32[512,8]{0,1:T(8,128)} %param.16) | copy-start | bytes 49156
  3.9 0.7 %copy-start.4 = (s32[512]{0:T(512)S(1)}, s32[512]{0:T(512)}, u32[]{:S(2)}) copy-start(s32[512]{0:T(512)} %param.13) | copy-start | bytes 6148
  4.6 0.7 %copy-start.5 = (f32[512]{0:T(512)S(1)}, f32[512]{0:T(512)}, u32[]{:S(2)}) copy-start(f32[512]{0:T(512)} %param.15) | copy-start | bytes 6148
  5.3 0.7 %copy-start.6 = (s32[16]{0:T(128)S(1)}, s32[16]{0:T(128)}, u32[]{:S(2)}) copy-start(s32[16]{0:T(128)} %tilt_ref.1) | copy-start | bytes 196
  5.9 0.7 %copy-start.7 = (s32[16]{0:T(128)S(1)}, s32[16]{0:T(128)}, u32[]{:S(2)}) copy-start(s32[16]{0:T(128)} %azi_ref.1) | copy-start | bytes 196
  6.6 0.8 %copy-start.8 = (bf16[128,256]{1,0:T(8,128)(2,1)S(1)}, bf16[128,256]{1,0:T(8,128)(2,1)}, u32[]{:S(2)}) copy-start(bf16[128,256]{1,0:T(8,128)(2,1)} %constant.7.ang_ref) | copy-start | bytes 196612
  7.4 0.8 %copy-start.9 = (f32[32,256]{1,0:T(8,128)S(1)}, f32[32,256]{1,0:T(8,128)}, u32[]{:S(2)}) copy-start(f32[32,256]{1,0:T(8,128)} %constant.4.clone.turn_ref) | copy-start | bytes 98308
